TPU v7x, 128 devices: a whole 4x4x4 slice. The times are simulated.
128 devices in a mesh: span: 16 (over x, y), expert: 8 (over z, core).
Axes of the slice: x: 4, y: 4, z: 4, core: 2. Of those that a mesh axis runs over, the one named last changes fastest.
Arguments:
- residual_in: bfloat16 [16384, 6144], P(('span', 'expert')), may hold values from -6 to 6
- queries: bfloat16 [16384, 4096], P('span', 'expert'), may hold values from -6 to 6
- key_rows: bfloat16 [16384, 4096], P('span', 'expert'), may hold values from -6 to 6
- values: bfloat16 [16384, 4096], P('span', 'expert'), may hold values from -6 to 6
- log_keep: float32 [16384, 32], P('span', 'expert'), may hold values from -0.52 to 0, as said below
- prompt_start: int32 [16], P('span'), may hold values from 1 to 1024, as said below
- out_proj: bfloat16 [4096, 6144], P('expert', 'span'), may hold values from -0.09375 to 0.09375
- norm_gain: float32 [6144], replicated, may hold values from 0.1 to 1.9
- expert_ids: int32 [16384, 1], P(('span', 'expert')), may hold values from 0 to 15; in each aligned block of 128 rows (0 to 127, 128 to 255, ...) at most 10 rows name the same one
- w_gate: bfloat16 [16, 6144, 5120], P('span', None, 'expert'), may hold values from -0.078125 to 0.078125
- w_up: bfloat16 [16, 6144, 5120], P('span', None, 'expert'), may hold values from -0.078125 to 0.078125
Outputs:
- hidden_state: bfloat16 [16384, 6144], P(('span', 'expert'))
- expert_hidden: bfloat16 [16, 1280, 5120], P('span', None, 'expert')
Inputs may be any that keep to these rules, and one draw needn't show every extreme that they name: `log_keep`: logarithm of a share of state kept, always below 0. `prompt_start`: position within its section of 1024 tokens at which a new prompt begins, 1024 where none does; exactly one section of the upper half of the 16 sections holds such a start. `expert_ids`: at most 10 of the 128 rows of one device name the same expert, and in every draw some device has exactly 10 rows naming one expert.
All inputs are finite; a program needn't handle non-finite values.
Results may differ from a plain program's by a relative error of at most 0.029.
Values may be sent and summed in bfloat16 or wider, within the bound.
No kernel may reach another device: no remote copies, remote signals or barrier semaphores. Data moves between devices by JAX's collectives and lax.ppermute only.
A program may use at most 192 MiB of HBM per device.

v0:
```python
import jax
import jax.numpy as jnp
from jax import lax
from jax.sharding import PartitionSpec as P

BLK = 512


EPSILON = 1e-05
HIGHEST = lax.Precision.HIGHEST


def shifted(block, axis, distance):
    devices = range(lax.axis_size(axis))
    route = [(i - distance, i) for i in devices if i - distance in devices]
    return lax.ppermute(block, axis, route)


def block_pass(carried, block_in):
    queries, key_rows, values, log_keep, doc_count, base_count = block_in
    cumulative = jnp.cumsum(log_keep, axis=0)
    cum_heads = cumulative.T
    token_places = jnp.arange(log_keep.shape[0])
    allowed = (token_places[:, None] >= token_places[None, :]) & (
        doc_count[:, None] == doc_count[None, :]
    )
    allowed = allowed[None, :, :]
    spread = cum_heads[:, :, None] - cum_heads[:, None, :]
    decay_factor = jnp.where(allowed, jnp.exp(jnp.where(allowed, spread, 0.0)), 0.0)
    scores = jnp.einsum("thd,shd->hts", queries, key_rows, preferred_element_type=jnp.float32)
    weights = (scores * decay_factor).astype(jnp.bfloat16)
    intra_part = jnp.einsum("hts,she->the", weights, values, preferred_element_type=jnp.float32)
    query_f = queries.astype(jnp.float32)
    key_f = key_rows.astype(jnp.float32)
    value_f = values.astype(jnp.float32)
    opened = jnp.where((doc_count == base_count)[:, None], jnp.exp(cumulative), 0.0)
    incoming = jnp.einsum("thd,hde->the", query_f, carried, precision=HIGHEST) * opened[:, :, None]
    last_count = doc_count[-1]
    tail_weight = jnp.where(
        (doc_count == last_count)[:, None], jnp.exp(cumulative[-1][None, :] - cumulative), 0.0
    )
    through = jnp.where(last_count == base_count, jnp.exp(cumulative[-1]), 0.0)
    added_state = jnp.einsum(
        "shd,she->hde", key_f * tail_weight[:, :, None], value_f, precision=HIGHEST
    )
    return (carried * through[:, None, None] + added_state, intra_part + incoming)


def swiglu_rows(rows_in, gate_w, up_w):
    gate_part = jnp.dot(rows_in, gate_w, preferred_element_type=jnp.float32)
    up_part = jnp.dot(rows_in, up_w, preferred_element_type=jnp.float32)
    return (jax.nn.silu(gate_part) * up_part).astype(jnp.bfloat16)


def on_device(
    residual_in,
    queries,
    key_rows,
    values,
    log_keep,
    prompt_start,
    out_proj,
    norm_gain,
    expert_ids,
    w_gate,
    w_up,
):
    tok_rows = residual_in.shape[0]
    model_width = residual_in.shape[1]
    section_len = queries.shape[0]
    head_count = log_keep.shape[1]
    head_dim = queries.shape[1] // head_count
    span_count = lax.axis_size("span")
    slice_count = lax.axis_size("expert")
    capacity = max(2, tok_rows * 5 // (4 * span_count))
    start_here = prompt_start[0]
    token_places = jnp.arange(section_len)
    doc_count = (token_places >= start_here).astype(jnp.int32)
    block_total = section_len // BLK
    base_count = (start_here < jnp.arange(block_total) * BLK).astype(jnp.int32)
    empty_state = jnp.zeros((head_count, head_dim, head_dim), jnp.float32)
    block_inputs = (
        queries.reshape(block_total, BLK, head_count, head_dim),
        key_rows.reshape(block_total, BLK, head_count, head_dim),
        values.reshape(block_total, BLK, head_count, head_dim),
        log_keep.reshape(block_total, BLK, head_count),
        doc_count.reshape(block_total, BLK),
        base_count,
    )
    local_state, outputs = lax.scan(block_pass, empty_state, block_inputs)
    local_out = outputs.reshape(section_len, head_count, head_dim)
    device_cum = jnp.cumsum(log_keep, axis=0)
    through = jnp.where(start_here >= section_len, jnp.exp(device_cum[-1]), 0.0)

    def relay_step(step_index, incoming_now):
        outgoing = incoming_now * through[:, None, None] + local_state
        return shifted(outgoing.astype(jnp.bfloat16), "span", 1).astype(outgoing.dtype)

    incoming = lax.fori_loop(0, span_count - 1, relay_step, empty_state)
    opened = jnp.where((doc_count == 0)[:, None], jnp.exp(device_cum), 0.0)
    query_f = queries.reshape(section_len, head_count, head_dim).astype(jnp.float32)
    attn_heads = (
        local_out
        + jnp.einsum("thd,hde->the", query_f, incoming, precision=HIGHEST) * opened[:, :, None]
    )
    normed = attn_heads * lax.rsqrt(
        jnp.mean(attn_heads * attn_heads, axis=2, keepdims=True) + EPSILON
    )
    normed = normed.astype(jnp.bfloat16).reshape(section_len, head_count * head_dim)
    proj_full = lax.all_gather(out_proj, "span", axis=1, tiled=True)
    attn_rows = lax.psum_scatter(
        jnp.dot(normed, proj_full, preferred_element_type=jnp.float32).astype(jnp.bfloat16),
        "expert",
        scatter_dimension=0,
        tiled=True,
    ).astype(jnp.float32)
    mixed = residual_in.astype(jnp.float32) + attn_rows
    hidden_state = mixed.astype(jnp.bfloat16)
    moe_in = (
        mixed * lax.rsqrt(jnp.mean(mixed * mixed, axis=1, keepdims=True) + EPSILON) * norm_gain
    ).astype(jnp.bfloat16)
    chosen = expert_ids[:, 0]
    onehot = (chosen[:, None] == jnp.arange(span_count)[None, :]).astype(jnp.int32)
    earlier_count = jnp.cumsum(onehot, axis=0) - onehot
    slot_index = jnp.sum(earlier_count * onehot, axis=1)
    target = chosen * capacity + slot_index
    placing = (jnp.arange(span_count * capacity)[:, None] == target[None, :]).astype(jnp.bfloat16)
    packed = jnp.dot(placing, moe_in, preferred_element_type=jnp.float32).astype(jnp.bfloat16)
    packed = packed.reshape(span_count, capacity, model_width)
    gate_w = w_gate[0]
    up_w = w_up[0]
    slice_width = gate_w.shape[1]
    copies = jnp.broadcast_to(packed[:, None], (span_count, slice_count, capacity, model_width))
    copies = copies.reshape(span_count * slice_count, capacity, model_width)
    arrived_items = lax.all_to_all(
        copies, ("span", "expert"), split_axis=0, concat_axis=0, tiled=True
    )
    flat_rows = arrived_items.reshape(-1, model_width)
    result_rows = swiglu_rows(flat_rows, gate_w, up_w)
    arrived = result_rows.reshape(arrived_items.shape[0], arrived_items.shape[1], slice_width)
    hidden_rows = arrived.reshape(span_count, slice_count, capacity, slice_width)
    hidden_rows = hidden_rows.transpose(1, 0, 2, 3).reshape(
        slice_count * span_count * capacity, slice_width
    )
    return (hidden_state, hidden_rows[None])


def solution(mesh):
    placed = (
        P(("span", "expert"), None),
        P("span", "expert"),
        P("span", "expert"),
        P("span", "expert"),
        P("span", "expert"),
        P("span"),
        P("expert", "span"),
        P(),
        P(("span", "expert"), None),
        P("span", None, "expert"),
        P("span", None, "expert"),
    )
    return jax.shard_map(
        on_device,
        mesh=mesh,
        in_specs=placed,
        out_specs=(P(("span", "expert"), None), P("span", None, "expert")),
        check_vma=False,
    )
```

profile of v0, /device:TPU:1, one launch (start us, length us, event | category | flops | bytes accessed | tf_op | source)
XLA Modules:
  0.0 697.9 jit_solution(14939065314474137926)
XLA Ops:
  15.8 68.2 %while.24 = (s32[]{:T(128)}, f32[4,128,128]{2,1,0:T(8,128)S(1)}, f32[2,512,4,128]{1,0,3,2:T(2,128)}, s32[2,512]{1,0:T(2,128)S(1)}, s32[2]{0:T(128)S(1)}, /*index...) while((s32[]{:T(128)}, f32[4,128,128]{2,1,0:T(8,128)S(1)}, ...), condition=%wide.region_3.4_spmd.clone, body=%wide.region_0.3_spmd.clone.sunk | while | flops 1349786624 | bytes 32959232 | solution.py:90
  24.9 2.9 fusion.55
  30.4 19.5 %dynamic_update_slice.6 = f32[2,512,4,128]{1,0,3,2:T(2,128)} dynamic-update-slice(f32[2,512,4,128]{1,0,3,2:T(2,128)} %get-tuple-element.272, f32[1,512,4,128]{1,0,3,2:T(1,128)S(1)} %copy.90, s32[]{:T(128)S(6)} %copy.95, s32[]{:T(128)} %constant.34.clone.1..sunk, s32[]{:T(128)} %constant.34.clone.1..sunk, s32[]{:T(128)} %constant.34.clone.1..sunk) | dynamic-update-slice | bytes 2097156 | tf_op jit(solution)/shard_map/while/body/jit(dynamic_update_index_in_dim)/dynamic_update_slice | solution.py:90
  58.9 2.9 fusion.55
  64.4 19.5 %dynamic_update_slice.6 = f32[2,512,4,128]{1,0,3,2:T(2,128)} dynamic-update-slice(f32[2,512,4,128]{1,0,3,2:T(2,128)} %get-tuple-element.272, f32[1,512,4,128]{1,0,3,2:T(1,128)S(1)} %copy.90, s32[]{:T(128)S(6)} %copy.95, s32[]{:T(128)} %constant.34.clone.1..sunk, s32[]{:T(128)} %constant.34.clone.1..sunk, s32[]{:T(128)} %constant.34.clone.1..sunk) | dynamic-update-slice | bytes 2097156 | tf_op jit(solution)/shard_map/while/body/jit(dynamic_update_index_in_dim)/dynamic_update_slice | solution.py:90
  84.0 3.1 reshape.180
  87.8 111.5 %while.25 = (s32[]{:T(128)}, f32[4,128,128]{2,1,0:T(8,128)S(1)}, f32[4]{0:T(128)S(1)}, f32[4,128,128]{2,1,0:T(8,128)S(1)}, s32[]{:T(128)}, /*index=5*/s32[]{:T(128)}) while((s32[]{:T(128)}, f32[4,128,128]{2,1,0:T(8,128)S(1)}, f32[4]{0:T(128)S(1)}, f32[4,128,128]{2,1,0:T(8,128)S(1)}, s32[]{:T(128)}, /*index=5*/s32[]{:T(128)}) %tuple.65), condition=%wide.region_7.8_spmd.clone, body=%wide.region_6.7_spmd.clone.sunk | while | flops 327683 | bytes 1572999 | solution.py:99
  87.9 4.1 collective-permute-start
  94.3 4.1 collective-permute-start
  100.5 3.8 collective-permute-start
  106.3 3.8 collective-permute-start
  112.2 3.8 collective-permute-start
  118.0 5.5 collective-permute-start
  125.6 5.9 collective-permute-start
  133.6 5.9 collective-permute-start
  141.8 6.2 collective-permute-start
  148.0 3.2 collective-permute-done
  151.4 5.9 collective-permute-start
  159.4 6.0 collective-permute-start
  167.4 5.7 collective-permute-start
  175.2 6.2 collective-permute-start
  183.5 5.9 collective-permute-start
  191.5 5.9 collective-permute-start
  202.2 12.6 %convolution_convert_fusion = bf16[1024,6144]{1,0:T(8,128)(2,1)} fusion(bf16[1024,512]{0,1:T(8,128)(2,1)S(1)} %bitcast.147, bf16[512,6144]{1,0:T(8,128)(2,1)} %all-gather.2.cloned.1.call-done), kind=kOutput, calls=%fused_computation.39 | convolution fusion | flops 6448742400 | bytes 19922944 | tf_op jit(solution)/shard_map/dot_general | solution.py:112
  215.9 98.7 %reduce-scatter.2.cloned.1.call-done = bf16[128,6144]{1,0:T(8,128)(2,1)} async-done(((bf16[1024,6144]{1,0:T(8,128)(2,1)}), bf16[128,6144]{1,0:T(8,128)(2,1)}) %reduce-scatter.2.cloned.1.call-update) | async-done | bytes 1572880 | tf_op jit(solution)/shard_map/reduce_scatter | solution.py:111
  314.6 3.2 multiply_reduce_fusion
  322.7 3.2 broadcast_in_dim.97
  325.9 297.6 %all_to_all.5 = bf16[128,10,6144]{2,1,0:T(8,128)(2,1)} all-to-all(bf16[128,10,6144]{2,1,0:T(8,128)(2,1)S(1)} %bitcast.142), channel_id=1, replica_groups=mesh['span'=16,'expert'=8] {'span','expert'}, dimensions={0} | all-to-all | bytes 31457280 | tf_op jit(solution)/shard_map/all_to_all | solution.py:135
  623.5 26.3 %reshape.186 = bf16[1280,6144]{1,0:T(8,128)(2,1)} reshape(bf16[128,10,6144]{2,1,0:T(8,128)(2,1)} %all_to_all.5) | data formatting | bytes 31457280 | tf_op jit(solution)/shard_map/reshape | solution.py:138
  649.8 16.5 %fusion.21 = f32[1280,640]{1,0:T(8,128)S(1)} fusion(bf16[1280,6144]{1,0:T(8,128)(2,1)} %reshape.186, bf16[1,6144,640]{2,1,0:T(8,128)(2,1)} %param.24), kind=kOutput, calls=%fused_computation.42 | convolution fusion | flops 10066329600 | bytes 26869760 | tf_op jit(solution)/shard_map/dot_general | solution.py:50
  666.3 16.5 %fusion.26 = bf16[1280,640]{1,0:T(8,128)(2,1)} fusion(bf16[1280,6144]{1,0:T(8,128)(2,1)S(1)} %copy-done, bf16[1,6144,640]{2,1,0:T(8,128)(2,1)} %param.25, f32[1280,640]{1,0:T(8,128)S(1)} %fusion.21), kind=kOutput, calls=%fused_computation.46 | convolution fusion | flops 10071244800 | bytes 28508160 | tf_op jit(solution)/shard_map/dot_general | solution.py:51
  687.1 4.0 broadcast_in_dim_reshape.4
  (161 shorter events, 71.3 us)
Async XLA Ops:
  7.2 195.0 %all-gather.2.cloned.1.call-start = ((), (), s32[]{:S(2)}) async-start(), calls=%async_computation.2 | async-start | bytes 6684672 | tf_op jit(solution)/shard_map/all_gather | solution.py:110
  7.9 306.7 %reduce-scatter.2.cloned.1.call-start = ((), (), s32[]{:S(2)}) async-start(), calls=%async_computation.3 | async-start | bytes 14155776 | tf_op jit(solution)/shard_map/reduce_scatter | solution.py:111
  10.9 3.8 copy-start.8
  11.9 3.9 copy-start.10
  15.8 7.3 %copy-start.3 = (bf16[2,512,4,128]{3,2,1,0:T(4,128)(2,1)}, bf16[2,512,4,128]{3,2,1,0:T(4,128)(2,1)S(1)}, u32[]{:S(2)}) copy-start(bf16[2,512,4,128]{3,2,1,0:T(4,128)(2,1)S(1)} %get-tuple-element.289) | copy-start | bytes 3145732 | tf_op jit(solution)/shard_map/while
  15.8 9.0 %copy-start.1 = (bf16[2,512,4,128]{3,2,1,0:T(4,128)(2,1)}, bf16[2,512,4,128]{3,2,1,0:T(4,128)(2,1)S(1)}, u32[]{:S(2)}) copy-start(bf16[2,512,4,128]{3,2,1,0:T(4,128)(2,1)S(1)} %get-tuple-element.290) | copy-start | bytes 3145732 | tf_op jit(solution)/shard_map/while
  28.4 21.5 %copy-start.2 = (bf16[2,512,4,128]{3,2,1,0:T(4,128)(2,1)S(1)}, bf16[2,512,4,128]{3,2,1,0:T(4,128)(2,1)}, u32[]{:S(2)}) copy-start(bf16[2,512,4,128]{3,2,1,0:T(4,128)(2,1)} %copy-done.1) | copy-start | bytes 3145732 | tf_op jit(solution)/shard_map/while
  28.4 21.5 %copy-start.4 = (bf16[2,512,4,128]{3,2,1,0:T(4,128)(2,1)S(1)}, bf16[2,512,4,128]{3,2,1,0:T(4,128)(2,1)}, u32[]{:S(2)}) copy-start(bf16[2,512,4,128]{3,2,1,0:T(4,128)(2,1)} %copy-done.3) | copy-start | bytes 3145732 | tf_op jit(solution)/shard_map/while
  49.9 7.3 %copy-start.3 = (bf16[2,512,4,128]{3,2,1,0:T(4,128)(2,1)}, bf16[2,512,4,128]{3,2,1,0:T(4,128)(2,1)S(1)}, u32[]{:S(2)}) copy-start(bf16[2,512,4,128]{3,2,1,0:T(4,128)(2,1)S(1)} %get-tuple-element.289) | copy-start | bytes 3145732 | tf_op jit(solution)/shard_map/while
  49.9 9.0 %copy-start.1 = (bf16[2,512,4,128]{3,2,1,0:T(4,128)(2,1)}, bf16[2,512,4,128]{3,2,1,0:T(4,128)(2,1)S(1)}, u32[]{:S(2)}) copy-start(bf16[2,512,4,128]{3,2,1,0:T(4,128)(2,1)S(1)} %get-tuple-element.290) | copy-start | bytes 3145732 | tf_op jit(solution)/shard_map/while
  62.5 21.5 %copy-start.2 = (bf16[2,512,4,128]{3,2,1,0:T(4,128)(2,1)S(1)}, bf16[2,512,4,128]{3,2,1,0:T(4,128)(2,1)}, u32[]{:S(2)}) copy-start(bf16[2,512,4,128]{3,2,1,0:T(4,128)(2,1)} %copy-done.1) | copy-start | bytes 3145732 | tf_op jit(solution)/shard_map/while
  62.5 21.5 %copy-start.4 = (bf16[2,512,4,128]{3,2,1,0:T(4,128)(2,1)S(1)}, bf16[2,512,4,128]{3,2,1,0:T(4,128)(2,1)}, u32[]{:S(2)}) copy-start(bf16[2,512,4,128]{3,2,1,0:T(4,128)(2,1)} %copy-done.3) | copy-start | bytes 3145732 | tf_op jit(solution)/shard_map/while
  84.0 3.8 copy-start.5
  87.9 6.2 collective-permute-start
  94.3 6.0 collective-permute-start
  100.5 5.7 collective-permute-start
  106.3 5.7 collective-permute-start
  112.2 5.7 collective-permute-start
  118.0 7.5 %collective-permute-start = (bf16[4,128,128]{2,1,0:T(8,128)(2,1)S(1)}, bf16[4,128,128]{2,1,0:T(8,128)(2,1)S(1)}, u32[]{:S(2)}, u32[]{:S(2)}) collective-permute-start(bf16[4,128,128]{2,1,0:T(8,128)(2,1)S(1)} %fusion.57), channel_id=1, source_target_pairs={{0,8},{8,16},{16,24},{24,32},{32,40},{40,48},{48,56},{56,64},{64,7... | collective-permute-start | bytes 393224 | tf_op jit(solution)/shard_map/while/body/eval_jaxpr/ppermute | solution.py:16
  125.6 7.8 %collective-permute-start = (bf16[4,128,128]{2,1,0:T(8,128)(2,1)S(1)}, bf16[4,128,128]{2,1,0:T(8,128)(2,1)S(1)}, u32[]{:S(2)}, u32[]{:S(2)}) collective-permute-start(bf16[4,128,128]{2,1,0:T(8,128)(2,1)S(1)} %fusion.57), channel_id=1, source_target_pairs={{0,8},{8,16},{16,24},{24,32},{32,40},{40,48},{48,56},{56,64},{64,7... | collective-permute-start | bytes 393224 | tf_op jit(solution)/shard_map/while/body/eval_jaxpr/ppermute | solution.py:16
  133.6 8.1 %collective-permute-start = (bf16[4,128,128]{2,1,0:T(8,128)(2,1)S(1)}, bf16[4,128,128]{2,1,0:T(8,128)(2,1)S(1)}, u32[]{:S(2)}, u32[]{:S(2)}) collective-permute-start(bf16[4,128,128]{2,1,0:T(8,128)(2,1)S(1)} %fusion.57), channel_id=1, source_target_pairs={{0,8},{8,16},{16,24},{24,32},{32,40},{40,48},{48,56},{56,64},{64,7... | collective-permute-start | bytes 393224 | tf_op jit(solution)/shard_map/while/body/eval_jaxpr/ppermute | solution.py:16
  141.8 9.4 %collective-permute-start = (bf16[4,128,128]{2,1,0:T(8,128)(2,1)S(1)}, bf16[4,128,128]{2,1,0:T(8,128)(2,1)S(1)}, u32[]{:S(2)}, u32[]{:S(2)}) collective-permute-start(bf16[4,128,128]{2,1,0:T(8,128)(2,1)S(1)} %fusion.57), channel_id=1, source_target_pairs={{0,8},{8,16},{16,24},{24,32},{32,40},{40,48},{48,56},{56,64},{64,7... | collective-permute-start | bytes 393224 | tf_op jit(solution)/shard_map/while/body/eval_jaxpr/ppermute | solution.py:16
  151.4 7.9 %collective-permute-start = (bf16[4,128,128]{2,1,0:T(8,128)(2,1)S(1)}, bf16[4,128,128]{2,1,0:T(8,128)(2,1)S(1)}, u32[]{:S(2)}, u32[]{:S(2)}) collective-permute-start(bf16[4,128,128]{2,1,0:T(8,128)(2,1)S(1)} %fusion.57), channel_id=1, source_target_pairs={{0,8},{8,16},{16,24},{24,32},{32,40},{40,48},{48,56},{56,64},{64,7... | collective-permute-start | bytes 393224 | tf_op jit(solution)/shard_map/while/body/eval_jaxpr/ppermute | solution.py:16
  159.4 7.9 %collective-permute-start = (bf16[4,128,128]{2,1,0:T(8,128)(2,1)S(1)}, bf16[4,128,128]{2,1,0:T(8,128)(2,1)S(1)}, u32[]{:S(2)}, u32[]{:S(2)}) collective-permute-start(bf16[4,128,128]{2,1,0:T(8,128)(2,1)S(1)} %fusion.57), channel_id=1, source_target_pairs={{0,8},{8,16},{16,24},{24,32},{32,40},{40,48},{48,56},{56,64},{64,7... | collective-permute-start | bytes 393224 | tf_op jit(solution)/shard_map/while/body/eval_jaxpr/ppermute | solution.py:16
  167.4 7.6 %collective-permute-start = (bf16[4,128,128]{2,1,0:T(8,128)(2,1)S(1)}, bf16[4,128,128]{2,1,0:T(8,128)(2,1)S(1)}, u32[]{:S(2)}, u32[]{:S(2)}) collective-permute-start(bf16[4,128,128]{2,1,0:T(8,128)(2,1)S(1)} %fusion.57), channel_id=1, source_target_pairs={{0,8},{8,16},{16,24},{24,32},{32,40},{40,48},{48,56},{56,64},{64,7... | collective-permute-start | bytes 393224 | tf_op jit(solution)/shard_map/while/body/eval_jaxpr/ppermute | solution.py:16
  175.2 8.2 %collective-permute-start = (bf16[4,128,128]{2,1,0:T(8,128)(2,1)S(1)}, bf16[4,128,128]{2,1,0:T(8,128)(2,1)S(1)}, u32[]{:S(2)}, u32[]{:S(2)}) collective-permute-start(bf16[4,128,128]{2,1,0:T(8,128)(2,1)S(1)} %fusion.57), channel_id=1, source_target_pairs={{0,8},{8,16},{16,24},{24,32},{32,40},{40,48},{48,56},{56,64},{64,7... | collective-permute-start | bytes 393224 | tf_op jit(solution)/shard_map/while/body/eval_jaxpr/ppermute | solution.py:16
  183.5 7.8 %collective-permute-start = (bf16[4,128,128]{2,1,0:T(8,128)(2,1)S(1)}, bf16[4,128,128]{2,1,0:T(8,128)(2,1)S(1)}, u32[]{:S(2)}, u32[]{:S(2)}) collective-permute-start(bf16[4,128,128]{2,1,0:T(8,128)(2,1)S(1)} %fusion.57), channel_id=1, source_target_pairs={{0,8},{8,16},{16,24},{24,32},{32,40},{40,48},{48,56},{56,64},{64,7... | collective-permute-start | bytes 393224 | tf_op jit(solution)/shard_map/while/body/eval_jaxpr/ppermute | solution.py:16
  191.5 7.8 %collective-permute-start = (bf16[4,128,128]{2,1,0:T(8,128)(2,1)S(1)}, bf16[4,128,128]{2,1,0:T(8,128)(2,1)S(1)}, u32[]{:S(2)}, u32[]{:S(2)}) collective-permute-start(bf16[4,128,128]{2,1,0:T(8,128)(2,1)S(1)} %fusion.57), channel_id=1, source_target_pairs={{0,8},{8,16},{16,24},{24,32},{32,40},{40,48},{48,56},{56,64},{64,7... | collective-permute-start | bytes 393224 | tf_op jit(solution)/shard_map/while/body/eval_jaxpr/ppermute | solution.py:16
  214.8 99.8 %copy-start.6 = (bf16[128,6144]{1,0:T(8,128)(2,1)S(1)}, bf16[128,6144]{1,0:T(8,128)(2,1)}, u32[]{:S(2)}) copy-start(bf16[128,6144]{1,0:T(8,128)(2,1)} %param.15) | copy-start | bytes 4718596
  214.8 103.0 %copy-start.11 = (f32[6144]{0:T(1024)S(1)}, f32[6144]{0:T(1024)}, u32[]{:S(2)}) copy-start(f32[6144]{0:T(1024)} %param.22) | copy-start | bytes 73732
  314.6 3.2 copy-start.7
  649.8 16.5 %copy-start = (bf16[1280,6144]{1,0:T(8,128)(2,1)S(1)}, bf16[1280,6144]{1,0:T(8,128)(2,1)}, u32[]{:S(2)}) copy-start(bf16[1280,6144]{1,0:T(8,128)(2,1)} %reshape.186) | copy-start | bytes 47185924
  (2 other events, 1.5 us)
Sparse Core Ops, SparseCore 0:
  10.1 69.9 all-gather.1
  214.9 99.6 reduce-scatter.1
where the time goes:
time: 702 us; the launch traced here: 698 us
  blocking collectives  298 us (42%)
  waiting for transfers between devices  130 us (19%)
  local copies, waits for them, and re-layouts  98.6 us (14%)
  starting transfers between devices  78.7 us (11%)
  matrix products  59.1 us (8%)
  other arithmetic  15.8 us (2%)
  between operations  14.9 us (2%)
    all_to_all x1, blocking collectives, on_device(): lax.all_to_all(copies, ('span', 'expert'), split_axis=0, concat_axis=0, t...  298 us
    reduce_scatter x1, waiting for transfers between devices, on_device(): lax.psum_scatter(jnp.dot(normed, proj_full, preferred_element_type=jnp.fl...  98.7 us
    ppermute x15, starting transfers between devices, shifted(): return lax.ppermute(block, axis, route)  78.6 us
    dynamic_update_slice x4, local copies, waits for them, and re-layouts, on_device(): local_state, outputs = lax.scan(block_pass, empty_state, block_inputs)  41.2 us
    ppermute x15, waiting for transfers between devices, shifted(): return lax.ppermute(block, axis, route)  30.6 us
    reshape x1, local copies, waits for them, and re-layouts, on_device(): flat_rows = arrived_items.reshape(-1, model_width)  26.3 us
    dot_general x1, matrix products, swiglu_rows(): up_part = jnp.dot(rows_in, up_w, preferred_element_type=jnp.float32)  16.5 us
    dot_general x1, matrix products, swiglu_rows(): gate_part = jnp.dot(rows_in, gate_w, preferred_element_type=jnp.float32)  16.5 us
  transfers between devices with their start and end apart: 17, of which 16 were waited for; matrix products, arithmetic and copies ran while one was open for 12% of the time, Pallas kernels for 0%

commit v1 on v0

v1 whole, which is shorter than its diff:
```python
import functools

import jax
import jax.numpy as jnp
from jax import lax
from jax.experimental import pallas as pl
from jax.experimental.pallas import tpu as pltpu
from jax.sharding import PartitionSpec as P

BLK = 512
EPSILON = 1e-05
HIGHEST = lax.Precision.HIGHEST
F32 = jnp.float32
BF16 = jnp.bfloat16
VMEM_LIMIT = 56 * 1024 * 1024
HEADS = 4
HD = 128
GRID_SIDE = 4


def whole(shape):
    return pl.BlockSpec(shape, lambda *_: (0,) * len(shape))


def smem():
    return pl.BlockSpec(memory_space=pltpu.SMEM)


def split_dot(a_f32, b_bf16):
    high = a_f32.astype(BF16)
    low = (a_f32 - high.astype(F32)).astype(BF16)
    return jnp.dot(high, b_bf16, preferred_element_type=F32) + jnp.dot(
        low, b_bf16, preferred_element_type=F32
    )


def state_kernel(start_ref, k_ref, v_ref, keep_ref, pay_ref, first_ref, thr_ref, cum_ref):
    start = start_ref[0]
    blocks = k_ref.shape[0] // BLK
    row = lax.broadcasted_iota(jnp.int32, (BLK, BLK), 0)
    col = lax.broadcasted_iota(jnp.int32, (BLK, BLK), 1)
    lower = (row >= col).astype(F32)
    place = lax.broadcasted_iota(jnp.int32, (BLK, HD), 0)
    through, tails = [], []
    for b in range(blocks):
        own = pl.ds(b * BLK, BLK)
        cum = jnp.dot(lower, keep_ref[own, :], precision=HIGHEST, preferred_element_type=F32)
        cum_ref[own, :] = cum
        end = cum[BLK - 1 :, :]
        here = start - b * BLK
        same = (place >= here) == (here <= BLK - 1)
        tails.append(jnp.where(same, jnp.exp(end - cum), 0.0))
        resets = (here >= 0) & (here < BLK)
        through.append(jnp.where(resets, 0.0, jnp.exp(end)))
    pay_ref[HEADS * HD :, :] = jnp.zeros_like(pay_ref[HEADS * HD :, :])
    thr_ref[...] = jnp.zeros_like(thr_ref)
    highs, lows = [], []
    for h in range(HEADS):
        lanes = slice(h * HD, (h + 1) * HD)
        state = None
        passed = jnp.ones((1, HD), F32)
        for b in range(blocks):
            own = pl.ds(b * BLK, BLK)
            key = k_ref[own, lanes].astype(F32) * tails[b][:, h : h + 1]
            added = split_dot(key.T, v_ref[own, lanes])
            thr = jnp.broadcast_to(through[b][:, h : h + 1], (1, HD))
            passed = passed * thr
            if b == 0:
                first_ref[lanes, :] = added
                thr_ref[h : h + 1, :] = thr
                state = added
            else:
                state = state * thr + added
        pay_ref[lanes, :] = state.astype(BF16)
        high = passed.astype(BF16)
        highs.append(high.astype(F32))
        lows.append(passed - high.astype(F32))
    none = jnp.zeros((8 - HEADS, HD), F32)
    pay_ref[HEADS * HD :, :] = jnp.concatenate(
        highs + [none] + lows + [none], axis=0
    ).astype(BF16)


def local_state(start, key_rows, values, keep_pad):
    tokens, width = key_rows.shape
    return pl.pallas_call(
        state_kernel,
        grid=(1,),
        in_specs=[smem(), whole((tokens, width)), whole((tokens, width)), whole((tokens, HD))],
        out_specs=[
            whole((width + 16, HD)),
            whole((width, HD)),
            whole((8, HD)),
            whole((tokens, HD)),
        ],
        out_shape=[
            jax.ShapeDtypeStruct((width + 16, HD), BF16),
            jax.ShapeDtypeStruct((width, HD), F32),
            jax.ShapeDtypeStruct((8, HD), F32),
            jax.ShapeDtypeStruct((tokens, HD), F32),
        ],
        compiler_params=pltpu.CompilerParams(vmem_limit_bytes=VMEM_LIMIT),
        cost_estimate=pl.CostEstimate(
            flops=2 * 10**9, bytes_accessed=4 * 10**6, transcendentals=10**5
        ),
        name="local_state",
    )(start, key_rows, values, keep_pad)


def intra_kernel(start_ref, q_ref, k_ref, v_ref, cum_ref, keep_t_ref, out_ref):
    start = start_ref[0]
    blocks = q_ref.shape[0] // BLK
    row = lax.broadcasted_iota(jnp.int32, (BLK, BLK), 0)
    col = lax.broadcasted_iota(jnp.int32, (BLK, BLK), 1)
    upper = (row <= col).astype(F32)
    part = BLK // 2
    for b in range(blocks):
        cum_t = jnp.dot(
            keep_t_ref[:, b * BLK : (b + 1) * BLK],
            upper,
            precision=HIGHEST,
            preferred_element_type=F32,
        )
        here = start - b * BLK
        for r in range(2):
            lo, n = r * part, (r + 1) * part
            t = lax.broadcasted_iota(jnp.int32, (part, n), 0) + lo
            s = lax.broadcasted_iota(jnp.int32, (part, n), 1)
            allowed = (t >= s) & ((s >= here) | (t < here))
            rows = pl.ds(b * BLK + lo, part)
            for h in range(HEADS):
                lanes = slice(h * HD, (h + 1) * HD)
                scores = lax.dot_general(
                    q_ref[rows, lanes],
                    k_ref[b * BLK : b * BLK + n, lanes],
                    (((1,), (1,)), ((), ())),
                    preferred_element_type=F32,
                )
                spread = cum_ref[rows, h : h + 1] - cum_t[h : h + 1, :n]
                decay = jnp.where(allowed, jnp.exp(jnp.where(allowed, spread, 0.0)), 0.0)
                weights = (scores * decay).astype(BF16)
                out_ref[rows, lanes] = jnp.dot(
                    weights, v_ref[b * BLK : b * BLK + n, lanes], preferred_element_type=F32
                )


def intra_part(start, queries, key_rows, values, cum, keep_t):
    tokens, width = queries.shape
    return pl.pallas_call(
        intra_kernel,
        grid=(1,),
        in_specs=[
            smem(),
            whole((tokens, width)),
            whole((tokens, width)),
            whole((tokens, width)),
            whole((tokens, HD)),
            whole((8, tokens)),
        ],
        out_specs=whole((tokens, width)),
        out_shape=jax.ShapeDtypeStruct((tokens, width), F32),
        compiler_params=pltpu.CompilerParams(vmem_limit_bytes=VMEM_LIMIT),
        cost_estimate=pl.CostEstimate(
            flops=8 * 10**9, bytes_accessed=6 * 10**6, transcendentals=2 * 10**6
        ),
        name="intra_part",
    )(start, queries, key_rows, values, cum, keep_t)


def passes_of(pay, h):
    base = HEADS * HD
    high = pay[base + h : base + h + 1, :].astype(F32)
    low = pay[base + 8 + h : base + 9 + h, :].astype(F32)
    return high + low


def row_kernel(place_ref, p0, p1, p2, p3, pay_ref, prefix_ref, through_ref):
    own = place_ref[0]
    parts = [p[...] for p in (p0, p1, p2, p3)]
    places = [lax.rem(own - d + GRID_SIDE, GRID_SIDE) for d in range(GRID_SIDE)]
    one = jnp.ones((1, HD), F32)
    through_ref[...] = jnp.zeros_like(through_ref)
    highs, lows = [], []
    for h in range(HEADS):
        lanes = slice(h * HD, (h + 1) * HD)
        thr = [passes_of(p, h) for p in parts]
        total = jnp.zeros((HD, HD), F32)
        prefix = jnp.zeros((HD, HD), F32)
        passed, before = one, one
        for d in range(GRID_SIDE):
            after, between = one, one
            for e in range(GRID_SIDE):
                if e == d:
                    continue
                later = places[e] > places[d]
                after = after * jnp.where(later, thr[e], one)
                between = between * jnp.where(later & (places[e] < own), thr[e], one)
            state = parts[d][lanes, :].astype(F32)
            total = total + state * after
            prefix = prefix + state * jnp.where(places[d] < own, between, 0.0 * one)
            passed = passed * thr[d]
            before = before * jnp.where(places[d] < own, thr[d], one)
        pay_ref[lanes, :] = total.astype(BF16)
        prefix_ref[lanes, :] = prefix
        through_ref[h : h + 1, :] = before
        high = passed.astype(BF16)
        highs.append(high.astype(F32))
        lows.append(passed - high.astype(F32))
    none = jnp.zeros((8 - HEADS, HD), F32)
    pay_ref[HEADS * HD :, :] = jnp.concatenate(
        highs + [none] + lows + [none], axis=0
    ).astype(BF16)


def row_states(place, parts):
    shape = parts[0].shape
    width = HEADS * HD
    return pl.pallas_call(
        row_kernel,
        grid=(1,),
        in_specs=[smem()] + [whole(shape)] * 4,
        out_specs=[whole(shape), whole((width, HD)), whole((8, HD))],
        out_shape=[
            jax.ShapeDtypeStruct(shape, BF16),
            jax.ShapeDtypeStruct((width, HD), F32),
            jax.ShapeDtypeStruct((8, HD), F32),
        ],
        cost_estimate=pl.CostEstimate(
            flops=10**6, bytes_accessed=10**6, transcendentals=0
        ),
        name="row_states",
    )(place, *parts)


def finish_kernel(
    start_ref, q_ref, intra_ref, cum_ref, e1, e2, e3, prefix_ref, before_ref, first_ref, thr_ref, out_ref
):
    start = start_ref[0]
    blocks = q_ref.shape[0] // BLK
    rows1, rows2, rows3 = e1[...], e2[...], e3[...]
    place = lax.broadcasted_iota(jnp.int32, (BLK, HD), 0)
    factors = []
    for b in range(blocks):
        here = start - b * BLK
        opened = (place < here) | (here < 0)
        factors.append(jnp.where(opened, jnp.exp(cum_ref[pl.ds(b * BLK, BLK), :]), 0.0))
    for h in range(HEADS):
        lanes = slice(h * HD, (h + 1) * HD)
        far = rows2[lanes, :].astype(F32) + passes_of(rows2, h) * rows3[lanes, :].astype(F32)
        earlier = rows1[lanes, :].astype(F32) + passes_of(rows1, h) * far
        state = prefix_ref[lanes, :] + before_ref[h : h + 1, :] * earlier
        for b in range(blocks):
            own = pl.ds(b * BLK, BLK)
            if b > 0:
                state = state * thr_ref[h : h + 1, :] + first_ref[lanes, :]
            high = state.astype(BF16)
            low = (state - high.astype(F32)).astype(BF16)
            q = q_ref[own, lanes]
            carried = jnp.dot(q, high, preferred_element_type=F32) + jnp.dot(
                q, low, preferred_element_type=F32
            )
            heads = intra_ref[own, lanes] + carried * factors[b][:, h : h + 1]
            mean = jnp.mean(heads * heads, axis=1, keepdims=True)
            out_ref[own, lanes] = (heads * lax.rsqrt(mean + EPSILON)).astype(BF16)


def finish(start, queries, intra, cum, rows, prefix, before, first, thr):
    tokens, width = queries.shape
    pay = rows[0].shape
    return pl.pallas_call(
        finish_kernel,
        grid=(1,),
        in_specs=[
            smem(),
            whole((tokens, width)),
            whole((tokens, width)),
            whole((tokens, HD)),
            whole(pay),
            whole(pay),
            whole(pay),
            whole((width, HD)),
            whole((8, HD)),
            whole((width, HD)),
            whole((8, HD)),
        ],
        out_specs=whole((tokens, width)),
        out_shape=jax.ShapeDtypeStruct((tokens, width), BF16),
        compiler_params=pltpu.CompilerParams(vmem_limit_bytes=VMEM_LIMIT),
        cost_estimate=pl.CostEstimate(
            flops=10**9, bytes_accessed=5 * 10**6, transcendentals=10**6
        ),
        name="finish",
    )(start, queries, intra, cum, *rows, prefix, before, first, thr)


def proj_kernel(count, src_ref, *refs):
    xs = refs[:count]
    w_ref, res_ref, gain_ref, h_ref, x_ref = refs[count:]
    tile = 256

    def rows_of(step, _):
        own = pl.ds(pl.multiple_of(step * tile, tile), tile)
        total = jnp.zeros((tile, w_ref.shape[1]), F32)
        for c in range(count):
            depth = xs[c].shape[1]
            at = pl.ds(pl.multiple_of(src_ref[c] * depth, depth), depth)
            total = total + jnp.dot(
                xs[c][own, :], w_ref[at, :], preferred_element_type=F32
            )
        mixed = res_ref[own, :].astype(F32) + total
        h_ref[own, :] = mixed.astype(BF16)
        x_ref[own, :] = (mixed * gain_ref[...]).astype(BF16)
        return 0

    lax.fori_loop(0, res_ref.shape[0] // tile, rows_of, 0)


def project(src, xs, weights, res, gain):
    tokens = res.shape[0]
    columns = weights.shape[1]
    part = 256
    block = lambda rows: pl.BlockSpec((rows, part), lambda n, s: (0, n))
    return pl.pallas_call(
        functools.partial(proj_kernel, len(xs)),
        grid_spec=pltpu.PrefetchScalarGridSpec(
            num_scalar_prefetch=1,
            grid=(columns // part,),
            in_specs=[whole(x.shape) for x in xs]
            + [block(weights.shape[0]), block(tokens), block(1)],
            out_specs=[block(tokens), block(tokens)],
        ),
        out_shape=[jax.ShapeDtypeStruct((tokens, columns), BF16)] * 2,
        compiler_params=pltpu.CompilerParams(vmem_limit_bytes=VMEM_LIMIT),
        cost_estimate=pl.CostEstimate(
            flops=2 * tokens * columns * weights.shape[0],
            bytes_accessed=20 * 10**6,
            transcendentals=0,
        ),
        name="project",
    )(src, *xs, weights, res, gain)


def expert_kernel(count, begins, ends, src_ref, *refs):
    xs = refs[:count]
    gates = refs[count : 2 * count]
    ups = refs[2 * count : 3 * count]
    inverses = refs[3 * count : 4 * count]
    rest = refs[4 * count :]
    rows = xs[0].shape[0]
    if begins:
        gate = jnp.zeros((rows, gates[0].shape[1]), F32)
        up = jnp.zeros_like(gate)
        squares = jnp.zeros((rows, HD), F32)
    else:
        gate, up, squares = (r[...] for r in rest[:3])
        rest = rest[3:]
    for c in range(count):
        x = xs[c][...]
        gate = gate + jnp.dot(x, gates[c][...], preferred_element_type=F32)
        up = up + jnp.dot(x, ups[c][...], preferred_element_type=F32)
        plain = x.astype(F32) * inverses[c][...]
        plain = plain * plain
        for lane in range(plain.shape[1] // HD):
            squares = squares + plain[:, lane * HD : (lane + 1) * HD]
    if ends:
        mean = jnp.sum(squares, axis=1, keepdims=True) / ends
        scale = lax.rsqrt(mean + EPSILON)
        gate, up = gate * scale, up * scale
        rest[0][...] = (gate / (1.0 + jnp.exp(-gate)) * up).astype(BF16)
    else:
        rest[0][...] = gate
        rest[1][...] = up
        rest[2][...] = squares


def expert_part(src, xs, gate_w, up_w, inverse, carried, ends=0):
    tokens = xs[0].shape[0]
    hidden = gate_w.shape[1]
    tile = 320
    rows = lambda columns: pl.BlockSpec((tile, columns), lambda n, s: (n, 0))
    w_specs, i_specs = [], []
    for c, x in enumerate(xs):
        depth = x.shape[1]
        w_specs.append(pl.BlockSpec((depth, hidden), lambda n, s, c=c: (s[c], 0)))
        i_specs.append(pl.BlockSpec((1, depth), lambda n, s, c=c: (0, s[c])))
    kept = [rows(hidden), rows(hidden), rows(HD)]
    if ends:
        out_specs = rows(hidden)
        out_shape = jax.ShapeDtypeStruct((tokens, hidden), BF16)
    else:
        out_specs = kept
        out_shape = [
            jax.ShapeDtypeStruct((tokens, hidden), F32),
            jax.ShapeDtypeStruct((tokens, hidden), F32),
            jax.ShapeDtypeStruct((tokens, HD), F32),
        ]
    count = len(xs)
    return pl.pallas_call(
        functools.partial(expert_kernel, count, carried is None, ends),
        grid_spec=pltpu.PrefetchScalarGridSpec(
            num_scalar_prefetch=1,
            grid=(tokens // tile,),
            in_specs=[rows(x.shape[1]) for x in xs]
            + w_specs
            + w_specs
            + i_specs
            + ([] if carried is None else kept),
            out_specs=out_specs,
        ),
        out_shape=out_shape,
        compiler_params=pltpu.CompilerParams(vmem_limit_bytes=VMEM_LIMIT),
        cost_estimate=pl.CostEstimate(
            flops=4 * tokens * hidden * sum(x.shape[1] for x in xs),
            bytes_accessed=22 * 10**6,
            transcendentals=0,
        ),
        name="expert_part",
    )(
        src,
        *xs,
        *([gate_w] * count),
        *([up_w] * count),
        *([inverse] * count),
        *(() if carried is None else carried),
    )


def moved(block, axis, place_to):
    count = lax.axis_size(axis)
    return lax.ppermute(block, axis, [(i, place_to(i)) for i in range(count)])


def along(block, steps, cross=0):
    count = lax.axis_size("expert")
    return moved(block, "expert", lambda j: ((j // 2 + steps) * 2 + (j % 2 ^ cross)) % count)


def gathered(block, me):
    count = lax.axis_size("expert")
    other = me + 1 - 2 * lax.rem(me, 2)
    half = block.shape[1] // 2
    below, above = along(block, 1), along(block, -1)
    own_other = along(block, 0, 1)
    opp_a, opp_b = along(below[:, :half], 1), along(above[:, half:], -1)
    below_other, above_other = along(below, 0, 1), along(above, 0, 1)
    opp_a_other, opp_b_other = along(opp_a, 0, 1), along(opp_b, 0, 1)
    at = lambda j, d: lax.rem(j + d + count, count)
    first = [(block, me), (own_other, other)]
    second = [(below, at(me, -2)), (above, at(me, 2))]
    third = [(below_other, at(other, -2)), (above_other, at(other, 2))]
    opp, opp_other = at(me, 4), at(other, 4)
    fourth = [
        (opp_a, 2 * opp),
        (opp_b, 2 * opp + 1),
        (opp_a_other, 2 * opp_other),
        (opp_b_other, 2 * opp_other + 1),
    ]
    return first, second, third, fourth


def unzip(pairs):
    return [x for x, _ in pairs], jnp.stack([s for _, s in pairs]).astype(jnp.int32)


def on_device(
    residual_in,
    queries,
    key_rows,
    values,
    log_keep,
    prompt_start,
    out_proj,
    norm_gain,
    expert_ids,
    w_gate,
    w_up,
):
    tok_rows, model_width = residual_in.shape
    section_len = queries.shape[0]
    span_count = lax.axis_size("span")
    slice_count = lax.axis_size("expert")
    capacity = max(2, tok_rows * 5 // (4 * span_count))
    my_span = lax.axis_index("span")
    my_slice = lax.axis_index("expert")
    columns = model_width // slice_count

    half_rows = out_proj.shape[0] // 2
    parity = lax.rem(my_span, 2)
    send_a = lax.dynamic_slice_in_dim(out_proj, parity * half_rows, half_rows, 0)
    send_b = lax.dynamic_slice_in_dim(out_proj, (1 - parity) * half_rows, half_rows, 0)

    def route(flip):
        pairs = []
        for i in range(span_count):
            for j in range(slice_count):
                half = (i % 2) ^ flip
                pairs.append((i * slice_count + j, (2 * j + half) * slice_count + i // 2))
        return pairs

    got_a = lax.ppermute(send_a, ("span", "expert"), route(0))
    got_b = lax.ppermute(send_b, ("span", "expert"), route(1))
    piece = jnp.where(
        parity == 0,
        jnp.concatenate([got_a, got_b], axis=1),
        jnp.concatenate([got_b, got_a], axis=1),
    )
    proj_w = lax.all_gather(piece, "span", axis=0, tiled=True)

    keep_pad = jnp.pad(log_keep, ((0, 0), (0, HD - log_keep.shape[1])))
    keep_t = jnp.pad(log_keep.T, ((0, 8 - log_keep.shape[1]), (0, 0)))
    pay, first, thr, cum = local_state(prompt_start, key_rows, values, keep_pad)
    side = GRID_SIDE
    in_row = [
        moved(pay, "span", lambda i, d=d: i // side * side + (i + d) % side)
        for d in range(1, side)
    ]
    intra = intra_part(prompt_start, queries, key_rows, values, cum, keep_t)
    place = lax.rem(my_span, side)[None].astype(jnp.int32)
    row_pay, prefix, before = row_states(place, [pay] + in_row)
    rows = [
        lax.ppermute(
            row_pay,
            "span",
            [(i, i + d * side) for i in range(span_count) if i + d * side < span_count],
        )
        for d in range(1, side)
    ]
    normed = finish(prompt_start, queries, intra, cum, rows, prefix, before, first, thr)

    res = lax.all_to_all(residual_in, "expert", split_axis=1, concat_axis=0, tiled=True)
    ids = jnp.broadcast_to(expert_ids[:, 0][None, :], (slice_count, tok_rows))
    ids = lax.all_to_all(ids, "expert", split_axis=0, concat_axis=0, tiled=True)
    onehot = (ids[:, :, None] == jnp.arange(span_count)[None, None, :]).astype(BF16)
    earlier = jnp.tril(jnp.ones((tok_rows, tok_rows), BF16), -1)
    earlier_count = jnp.einsum("ts,bse->bte", earlier, onehot, preferred_element_type=F32)
    slot = jnp.sum(earlier_count * onehot.astype(F32), axis=2).astype(jnp.int32)
    block_of = jnp.arange(slice_count)[:, None]
    target = ((ids * slice_count + block_of) * capacity + slot).reshape(-1)
    slots = span_count * slice_count * capacity
    placing = (jnp.arange(slots)[:, None] == target[None, :]).astype(BF16)

    chunks = sum((list(g) for g in gathered(normed, my_slice)), [])
    xs, src = unzip(chunks)
    gain_cols = lax.dynamic_slice_in_dim(norm_gain, my_slice * columns, columns)[None, :]
    hidden_cols, rows_in = project(src, xs, proj_w, res, gain_cols)
    hidden_state = lax.all_to_all(
        hidden_cols, "expert", split_axis=0, concat_axis=1, tiled=True
    )

    packed = jnp.dot(placing, rows_in, preferred_element_type=F32).astype(BF16)
    packed = packed.reshape(span_count, slice_count * capacity, columns)
    arrived = lax.all_to_all(packed, "span", split_axis=0, concat_axis=0, tiled=True)
    arrived = arrived.reshape(slots, columns)
    inverse = (1.0 / norm_gain)[None, :]
    gate_w, up_w = w_gate[0], w_up[0]
    carried = None
    groups = gathered(arrived, my_slice)
    for number, group in enumerate(groups):
        xs, src = unzip(group)
        ends = model_width if number == len(groups) - 1 else 0
        carried = expert_part(src, xs, gate_w, up_w, inverse, carried, ends)
    r = jnp.arange(slots)
    block, rest = r // (span_count * capacity), r % (span_count * capacity)
    wanted = (rest // capacity * slice_count + block) * capacity + rest % capacity
    turning = (wanted[:, None] == r[None, :]).astype(BF16)
    hidden_rows = jnp.dot(turning, carried, preferred_element_type=F32).astype(BF16)
    return (hidden_state, hidden_rows[None])


def solution(mesh):
    placed = (
        P(("span", "expert"), None),
        P("span", "expert"),
        P("span", "expert"),
        P("span", "expert"),
        P("span", "expert"),
        P("span"),
        P("expert", "span"),
        P(),
        P(("span", "expert"), None),
        P("span", None, "expert"),
        P("span", None, "expert"),
    )
    return jax.shard_map(
        on_device,
        mesh=mesh,
        in_specs=placed,
        out_specs=(P(("span", "expert"), None), P("span", None, "expert")),
        check_vma=False,
    )
```

time: 702 us -> 351 us (0.50)
  blocking collectives: 298 us -> 30.6 us
  Pallas kernels: 0 us -> 84.5 us
  local copies, waits for them, and re-layouts: 98.6 us -> 18.1 us
  matrix products: 59.1 us -> 9.64 us
  waiting for transfers between devices: 130 us -> 114 us
  other arithmetic: 15.8 us -> 3.97 us
    all_to_all x1, blocking collectives: 298 us -> 30.6 us  [on_device(): lax.all_to_all(packed, 'span', split_axis=0, concat_axis=0, tiled=True)]
    reduce_scatter x1 -> x0, waiting for transfers between devices: 98.7 us -> none  [on_device(): lax.psum_scatter(jnp.dot(normed, proj_full, preferred_element_type=jnp.fl...]
    pallas_call x0 -> x9, Pallas kernels: none -> 84.5 us  [the longest x4 49.9 us: expert_part(): pl.pallas_call(functools.partial(expert_kernel, count, carried is None, e...]
    ppermute x15 -> x26, waiting for transfers between devices: 30.6 us -> 96.7 us  [the longest x21 86.7 us: moved(): return lax.ppermute(block, axis, [(i, place_to(i)) for i in range(count)])]
    dot_general x11 -> x3, matrix products: 59.1 us -> 9.64 us  [the longest x1 5.59 us: on_device(): jnp.dot(turning, carried, preferred_element_type=F32).astype(BF16)]
    dynamic_update_slice x4 -> x0, local copies, waits for them, and re-layouts: 41.2 us -> none  [on_device(): local_state, outputs = lax.scan(block_pass, empty_state, block_inputs)]
    reshape x7 -> x0, local copies, waits for them, and re-layouts: 33.3 us -> none  [the longest x1 26.3 us: on_device(): flat_rows = arrived_items.reshape(-1, model_width)]
    ppermute x15 -> x26, starting transfers between devices: 78.6 us -> 61.5 us  [the longest x3 27.7 us: on_device(): lax.ppermute(row_pay, 'span', [(i, i + d * side) for i in range(span_coun...]
  transfers between devices with their start and end apart: 17 -> 30, of which waited for: 16 -> 9; matrix products, arithmetic and copies ran while one was open for 12% -> 5% of each run, Pallas kernels for 0% -> 16%
where the time goes in v1:
time: 351 us; the launch traced here: 350 us
  waiting for transfers between devices  114 us (32%)
  Pallas kernels  84.5 us (24%)
  starting transfers between devices  75.1 us (21%)
  blocking collectives  30.6 us (9%)
  local copies, waits for them, and re-layouts  18.1 us (5%)
  between operations  15 us (4%)
  matrix products  9.64 us (3%)
  other arithmetic  3.97 us (1%)
    ppermute x21, waiting for transfers between devices, moved(): return lax.ppermute(block, axis, [(i, place_to(i)) for i in range(count)])  86.7 us
    pallas_call x4, Pallas kernels, expert_part(): pl.pallas_call(functools.partial(expert_kernel, count, carried is None, e...  49.9 us
    all_to_all x1, blocking collectives, on_device(): lax.all_to_all(packed, 'span', split_axis=0, concat_axis=0, tiled=True)  30.6 us
    ppermute x3, starting transfers between devices, on_device(): lax.ppermute(row_pay, 'span', [(i, i + d * side) for i in range(span_coun...  27.7 us
    ppermute x21, starting transfers between devices, moved(): return lax.ppermute(block, axis, [(i, place_to(i)) for i in range(count)])  26.9 us
    all_to_all x1, waiting for transfers between devices, on_device(): ids = lax.all_to_all(ids, 'expert', split_axis=0, concat_axis=0, tiled=True)  16.9 us
    pallas_call x1, Pallas kernels, project(): pl.pallas_call(functools.partial(proj_kernel, len(xs)), grid_spec=pltpu.P...  14.7 us
    slice x4, local copies, waits for them, and re-layouts, gathered(): opp_a, opp_b = (along(below[:, :half], 1), along(above[:, half:], -1))  7.49 us
  transfers between devices with their start and end apart: 30, of which 9 were waited for; matrix products, arithmetic and copies ran while one was open for 5% of the time, Pallas kernels for 16%

profile of v1, /device:TPU:1, one launch (start us, length us, event | category | flops | bytes accessed | tf_op | source)
XLA Modules:
  0.0 350.4 jit_solution(12324081943021694507)
XLA Ops:
  8.3 6.2 %collective-permute-start.15 = (bf16[256,384]{1,0:T(8,128)(2,1)S(1)}, bf16[256,384]{1,0:T(8,128)(2,1)S(1)}, u32[]{:S(2)}, u32[]{:S(2)}) collective-permute-start(bf16[256,384]{1,0:T(8,128)(2,1)S(1)} %get-tuple-element.38), channel_id=1, source_target_pairs={{0,0},{1,16},{2,32},{3,48},{4,64},{5,80},{6,96},{7,112},{8,8},{9,2... | collective-permute-start | bytes 589832 | tf_op jit(solution)/shard_map/ppermute | solution.py:500
  15.1 5.3 %collective-permute-done.15 = bf16[256,384]{1,0:T(8,128)(2,1)S(1)} collective-permute-done((bf16[256,384]{1,0:T(8,128)(2,1)S(1)}, bf16[256,384]{1,0:T(8,128)(2,1)S(1)}, u32[]{:S(2)}, u32[]{:S(2)}) %collective-permute-start.15) | collective-permute-done | bytes 196640 | tf_op jit(solution)/shard_map/ppermute | solution.py:500
  20.4 4.7 %collective-permute-done.16 = bf16[256,384]{1,0:T(8,128)(2,1)S(1)} collective-permute-done((bf16[256,384]{1,0:T(8,128)(2,1)S(1)}, bf16[256,384]{1,0:T(8,128)(2,1)S(1)}, u32[]{:S(2)}, u32[]{:S(2)}) %collective-permute-start.16) | collective-permute-done | bytes 196640 | tf_op jit(solution)/shard_map/ppermute | solution.py:501
  27.7 5.6 %local_state.1 = (bf16[528,128]{1,0:T(8,128)(2,1)}, f32[512,128]{1,0:T(8,128)}, f32[8,128]{1,0:T(8,128)}, f32[1024,128]{1,0:T(8,128)}) custom-call(s32[1]{0:T(128)S(6)} %copy.23.start_ref, bf16[1024,512]{1,0:T(8,128)(2,1)} %k_ref.3, bf16[1024,512]{1,0:T(8,128)(2,1)} %v_ref.3, f32[1024,128]{1,0:T(8,128)} %pad.8.keep_ref), custom_call_target="tpu_custom_call" | custom-call | flops 2000000000 | bytes 4000000 | tf_op jit(solution)/shard_map/local_state/pallas_call | solution.py:86
  33.3 2.7 collective-permute-start.2
  36.5 6.2 %collective-permute-done.p1 = bf16[528,128]{1,0:T(8,128)(2,1)S(1)} collective-permute-done((bf16[528,128]{1,0:T(8,128)(2,1)}, bf16[528,128]{1,0:T(8,128)(2,1)S(1)}, u32[]{:S(2)}, u32[]{:S(2)}) %collective-permute-start) | collective-permute-done | bytes 135200 | tf_op jit(solution)/shard_map/ppermute | solution.py:430
  45.4 8.7 %collective-permute-start.3 = (bf16[528,128]{1,0:T(8,128)(2,1)}, bf16[528,128]{1,0:T(8,128)(2,1)S(1)}, u32[]{:S(2)}, u32[]{:S(2)}) collective-permute-start(bf16[528,128]{1,0:T(8,128)(2,1)} %get-tuple-element.22), channel_id=1, source_target_pairs={{0,32},{8,40},{16,48},{24,56},{32,64},{40,72},{48,80},{56,88},{64,... | collective-permute-start | bytes 405512 | tf_op jit(solution)/shard_map/ppermute | solution.py:521
  54.2 17.7 %collective-permute-start.4 = (bf16[528,128]{1,0:T(8,128)(2,1)}, bf16[528,128]{1,0:T(8,128)(2,1)S(1)}, u32[]{:S(2)}, u32[]{:S(2)}) collective-permute-start(bf16[528,128]{1,0:T(8,128)(2,1)} %get-tuple-element.22), channel_id=1, source_target_pairs={{0,64},{8,72},{16,80},{24,88},{32,96},{40,104},{48,112},{56,120},{... | collective-permute-start | bytes 405512 | tf_op jit(solution)/shard_map/ppermute | solution.py:521
  73.2 7.1 %intra_part.1.intra_ref = f32[1024,512]{1,0:T(8,128)} custom-call(s32[1]{0:T(128)S(6)} %copy.23.start_ref, bf16[1024,512]{1,0:T(8,128)(2,1)} %q_ref.3, bf16[1024,512]{1,0:T(8,128)(2,1)} %k_ref.3, bf16[1024,512]{1,0:T(8,128)(2,1)} %v_ref.3, f32[1024,128]{1,0:T(8,128)} %get-tuple-element.20.cum_ref, f32[8,1024]{1,0:T(8,128)} %pad.9.keep_t_ref), custom_call_target="tpu_custom_call" | custom-call | flops 8000000000 | bytes 6000000 | tf_op jit(solution)/shard_map/intra_part/pallas_call | solution.py:149
  81.1 5.2 %finish.1.refs_0_ = bf16[1024,512]{1,0:T(8,128)(2,1)} custom-call(s32[1]{0:T(128)S(6)} %copy.23.start_ref, bf16[1024,512]{1,0:T(8,128)(2,1)} %q_ref.3, f32[1024,512]{1,0:T(8,128)} %intra_part.1.intra_ref, f32[1024,128]{1,0:T(8,128)} %get-tuple-element.20.cum_ref, bf16[528,128]{1,0:T(8,128)(2,1)} %copy-done.8, bf16[528,128]{1,0:T(8,128)(2,1)} %copy-done.10, ...), custom_call_target="tpu_custom_call" | custom-call | flops 1000000000 | bytes 5000000 | tf_op jit(solution)/shard_map/finish/pallas_call | solution.py:270
  86.3 2.7 collective-permute-start.8
  89.6 5.3 %all-to-all-start.2 = ((s32[8,1,128]{2,1,0:T(1,128)}), s32[8,1,128]{2,1,0:T(1,128)S(1)}, u32[]{:S(2)}, u32[]{:S(2)}) async-start(s32[8,1,128]{2,1,0:T(1,128)} %broadcast_in_dim.35), calls=%async_computation.2 | async-start | bytes 8192 | tf_op jit(solution)/shard_map/all_to_all | solution.py:532
  96.1 16.9 %all-to-all-done.2 = s32[8,1,128]{2,1,0:T(1,128)S(1)} async-done(((s32[8,1,128]{2,1,0:T(1,128)}), s32[8,1,128]{2,1,0:T(1,128)S(1)}, u32[]{:S(2)}, u32[]{:S(2)}) %all-to-all-start.2) | async-done | bytes 4128 | tf_op jit(solution)/shard_map/all_to_all | solution.py:532
  113.1 4.8 %all-to-all-start = ((bf16[128,8,768]{2,0,1:T(8,128)(2,1)}), bf16[128,8,768]{2,0,1:T(8,128)(2,1)S(1)}, u32[]{:S(2)}, u32[]{:S(2)}) async-start(bf16[128,8,768]{2,0,1:T(8,128)(2,1)} %bitcast.51), calls=%async_computation | async-start | bytes 3145728 | tf_op jit(solution)/shard_map/all_to_all | solution.py:530
  126.6 23.2 %collective-permute-done.11.refs_6_ = bf16[1024,256]{1,0:T(8,128)(2,1)} collective-permute-done((bf16[1024,256]{1,0:T(8,128)(2,1)S(1)}, bf16[1024,256]{1,0:T(8,128)(2,1)}, u32[]{:S(2)}, u32[]{:S(2)}) %collective-permute-start.11) | collective-permute-done | bytes 524320 | tf_op jit(solution)/shard_map/ppermute | solution.py:430
  153.1 14.7 %project.1 = (bf16[1024,768]{1,0:T(8,128)(2,1)}, bf16[1024,768]{1,0:T(8,128)(2,1)}) custom-call(s32[10]{0:T(128)} %stack.65.src_ref, bf16[1024,512]{1,0:T(8,128)(2,1)} %finish.1.refs_0_, bf16[1024,512]{1,0:T(8,128)(2,1)} %collective-permute-done.6.refs_1_, bf16[1024,512]{1,0:T(8,128)(2,1)} %collective-permute-done.7.refs_2_, ...), custom_call_target="tpu_custom_call" | custom-call | flops 6442450944 | bytes 20000000 | tf_op jit(solution)/shard_map/project/pallas_call | solution.py:323
  167.8 3.8 %fusion.2 = bf16[1280,768]{1,0:T(8,128)(2,1)S(1)} fusion(bf16[1024,768]{1,0:T(8,128)(2,1)} %get-tuple-element.28, s32[1024]{0:T(1024)S(1)} %bitcast_add_fusion), kind=kOutput, calls=%fused_computation.4 | convolution fusion | flops 2015559680 | bytes 3543040 | tf_op jit(solution)/shard_map/dot_general | solution.py:550
  171.7 30.6 %all_to_all.49 = bf16[16,80,768]{2,1,0:T(8,128)(2,1)S(1)} all-to-all(bf16[16,80,768]{2,1,0:T(8,128)(2,1)S(1)} %bitcast.87), channel_id=1, replica_groups=mesh['span'=16,'expert'=8] {'span'}, dimensions={0} | all-to-all | bytes 3932160 | tf_op jit(solution)/shard_map/all_to_all | solution.py:552
  202.2 2.7 collective-permute-start.19
  204.9 2.9 collective-permute-start.25
  207.8 3.5 %all-to-all-start.1 = ((bf16[8,128,768]{2,1,0:T(8,128)(2,1)}), bf16[8,128,768]{2,1,0:T(8,128)(2,1)S(1)}, u32[]{:S(2)}, u32[]{:S(2)}) async-start(bf16[8,128,768]{2,1,0:T(8,128)(2,1)} %bitcast.91), calls=%async_computation.1 | async-start | bytes 3145728 | tf_op jit(solution)/shard_map/all_to_all | solution.py:546
  211.4 35.0 %collective-permute-done.17.refs_0_ = bf16[1280,768]{1,0:T(8,128)(2,1)} collective-permute-done((bf16[1280,768]{1,0:T(8,128)(2,1)S(1)}, bf16[1280,768]{1,0:T(8,128)(2,1)}, u32[]{:S(2)}, u32[]{:S(2)}) %collective-permute-start.17) | collective-permute-done | bytes 1966112 | tf_op jit(solution)/shard_map/ppermute | solution.py:430
  246.4 7.4 %collective-permute-start.23 = (bf16[1280,768]{1,0:T(8,128)(2,1)}, bf16[1280,768]{1,0:T(8,128)(2,1)}, u32[]{:S(2)}, u32[]{:S(2)}) collective-permute-start(bf16[1280,768]{1,0:T(8,128)(2,1)} %collective-permute-done.17.refs_0_), channel_id=1, source_target_pairs={{0,1},{1,0},{2,3},{3,2},{4,5},{5,4},{6,7},{7,6},{8,9},{9,8},{10,11... | collective-permute-start | bytes 5898248 | tf_op jit(solution)/shard_map/ppermute | solution.py:430
  253.8 2.2 slice.18
  256.0 2.3 slice.19
  258.3 2.9 collective-permute-start.20
  265.7 19.9 %collective-permute-done.18.refs_0_ = bf16[1280,384]{1,0:T(8,128)(2,1)} collective-permute-done((bf16[1280,384]{1,0:T(8,128)(2,1)}, bf16[1280,384]{1,0:T(8,128)(2,1)}, u32[]{:S(2)}, u32[]{:S(2)}) %collective-permute-start.18) | collective-permute-done | bytes 983072 | tf_op jit(solution)/shard_map/ppermute | solution.py:430
  286.7 11.0 %expert_part.4 = (f32[1280,640]{1,0:T(8,128)}, f32[1280,640]{1,0:T(8,128)}, f32[1280,128]{1,0:T(8,128)}) custom-call(s32[2]{0:T(128)} %pad_add_fusion.3.src_ref, bf16[1280,768]{1,0:T(8,128)(2,1)} %bitcast.75, bf16[1280,768]{1,0:T(8,128)(2,1)} %collective-permute-done.25.refs_1_, bf16[6144,640]{1,0:T(8,128)(2,1)} %bitcast.52, bf16[6144,640]{1,0:T(8,128)(2,1)} %bitcast.53, ...), custom_call_target="tpu_custom_call" | custom-call | flops 5033164800 | bytes 22000000 | tf_op jit(solution)/shard_map/expert_part/pallas_call | solution.py:398
  297.8 12.4 %expert_part.5 = (f32[1280,640]{1,0:T(8,128)}, f32[1280,640]{1,0:T(8,128)}, f32[1280,128]{1,0:T(8,128)}) custom-call(s32[2]{0:T(128)} %pad_add_fusion.2.src_ref, bf16[1280,768]{1,0:T(8,128)(2,1)} %collective-permute-done.17.refs_0_, bf16[1280,768]{1,0:T(8,128)(2,1)} %collective-permute-done.19.refs_1_, bf16[6144,640]{1,0:T(8,128)(2,1)} %bitcast.54, ...), custom_call_target="tpu_custom_call" | custom-call | flops 5033164800 | bytes 22000000 | tf_op jit(solution)/shard_map/expert_part/pallas_call | solution.py:398
  310.2 12.4 %expert_part.6 = (f32[1280,640]{1,0:T(8,128)}, f32[1280,640]{1,0:T(8,128)}, f32[1280,128]{1,0:T(8,128)}) custom-call(s32[2]{0:T(128)} %pad_add_fusion.1.src_ref, bf16[1280,768]{1,0:T(8,128)(2,1)} %collective-permute-done.23.refs_0_, bf16[1280,768]{1,0:T(8,128)(2,1)} %collective-permute-done.24.refs_1_, bf16[6144,640]{1,0:T(8,128)(2,1)} %bitcast.56, ...), custom_call_target="tpu_custom_call" | custom-call | flops 5033164800 | bytes 22000000 | tf_op jit(solution)/shard_map/expert_part/pallas_call | solution.py:398
  323.9 14.0 %expert_part.7 = bf16[1280,640]{1,0:T(8,128)(2,1)} custom-call(s32[4]{0:T(128)} %pad_add_fusion.src_ref, bf16[1280,384]{1,0:T(8,128)(2,1)} %collective-permute-done.18.refs_0_, bf16[1280,384]{1,0:T(8,128)(2,1)} %collective-permute-done.20.refs_1_, bf16[1280,384]{1,0:T(8,128)(2,1)} %copy-done.4, bf16[1280,384]{1,0:T(8,128)(2,1)} %copy-done.5, ...), custom_call_target="tpu_custom_call" | custom-call | flops 5033164800 | bytes 22000000 | tf_op jit(solution)/shard_map/expert_part/pallas_call | solution.py:398
  337.9 5.6 %fusion.5 = bf16[1,1280,640]{2,1,0:T(8,128)(2,1)} fusion(bf16[1280,640]{1,0:T(8,128)(2,1)} %expert_part.7, s32[1280]{0:T(1024)S(1)} %fusion.25), kind=kOutput, calls=%fused_computation.7 | convolution fusion | flops 2099609600 | bytes 3281920 | tf_op jit(solution)/shard_map/dot_general | solution.py:566
  (96 shorter events, 29.7 us)
Async XLA Ops:
  7.2 145.9 %all-gather.2.cloned.1.call-start = ((), (), s32[]{:S(2)}) async-start(), calls=%async_computation.4 | async-start | bytes 6684672 | tf_op jit(solution)/shard_map/all_gather | solution.py:507
  8.3 12.1 %collective-permute-start.15 = (bf16[256,384]{1,0:T(8,128)(2,1)S(1)}, bf16[256,384]{1,0:T(8,128)(2,1)S(1)}, u32[]{:S(2)}, u32[]{:S(2)}) collective-permute-start(bf16[256,384]{1,0:T(8,128)(2,1)S(1)} %get-tuple-element.38), channel_id=1, source_target_pairs={{0,0},{1,16},{2,32},{3,48},{4,64},{5,80},{6,96},{7,112},{8,8},{9,2... | collective-permute-start | bytes 589832 | tf_op jit(solution)/shard_map/ppermute | solution.py:500
  14.5 10.5 %collective-permute-start.16 = (bf16[256,384]{1,0:T(8,128)(2,1)S(1)}, bf16[256,384]{1,0:T(8,128)(2,1)S(1)}, u32[]{:S(2)}, u32[]{:S(2)}) collective-permute-start(bf16[256,384]{1,0:T(8,128)(2,1)S(1)} %get-tuple-element.39), channel_id=1, source_target_pairs={{0,8},{1,24},{2,40},{3,56},{4,72},{5,88},{6,104},{7,120},{8,0},{9,... | collective-permute-start | bytes 589832 | tf_op jit(solution)/shard_map/ppermute | solution.py:501
  33.3 9.5 %collective-permute-start = (bf16[528,128]{1,0:T(8,128)(2,1)}, bf16[528,128]{1,0:T(8,128)(2,1)S(1)}, u32[]{:S(2)}, u32[]{:S(2)}) collective-permute-start(bf16[528,128]{1,0:T(8,128)(2,1)} %get-tuple-element.21.p0), channel_id=1, source_target_pairs={{0,8},{8,16},{16,24},{24,0},{32,40},{40,48},{48,56},{56,32},{64,72... | collective-permute-start | bytes 405512 | tf_op jit(solution)/shard_map/ppermute | solution.py:430
  33.3 9.5 %collective-permute-start.1 = (bf16[528,128]{1,0:T(8,128)(2,1)}, bf16[528,128]{1,0:T(8,128)(2,1)S(1)}, u32[]{:S(2)}, u32[]{:S(2)}) collective-permute-start(bf16[528,128]{1,0:T(8,128)(2,1)} %get-tuple-element.21.p0), channel_id=1, source_target_pairs={{0,16},{8,24},{16,0},{24,8},{32,48},{40,56},{48,32},{56,40},{64,80... | collective-permute-start | bytes 405512 | tf_op jit(solution)/shard_map/ppermute | solution.py:430
  33.3 9.5 %collective-permute-start.2 = (bf16[528,128]{1,0:T(8,128)(2,1)}, bf16[528,128]{1,0:T(8,128)(2,1)S(1)}, u32[]{:S(2)}, u32[]{:S(2)}) collective-permute-start(bf16[528,128]{1,0:T(8,128)(2,1)} %get-tuple-element.21.p0), channel_id=1, source_target_pairs={{0,24},{8,0},{16,8},{24,16},{32,56},{40,32},{48,40},{56,48},{64,88... | collective-permute-start | bytes 405512 | tf_op jit(solution)/shard_map/ppermute | solution.py:430
  45.4 34.9 %collective-permute-start.3 = (bf16[528,128]{1,0:T(8,128)(2,1)}, bf16[528,128]{1,0:T(8,128)(2,1)S(1)}, u32[]{:S(2)}, u32[]{:S(2)}) collective-permute-start(bf16[528,128]{1,0:T(8,128)(2,1)} %get-tuple-element.22), channel_id=1, source_target_pairs={{0,32},{8,40},{16,48},{24,56},{32,64},{40,72},{48,80},{56,88},{64,... | collective-permute-start | bytes 405512 | tf_op jit(solution)/shard_map/ppermute | solution.py:521
  54.2 26.1 %collective-permute-start.4 = (bf16[528,128]{1,0:T(8,128)(2,1)}, bf16[528,128]{1,0:T(8,128)(2,1)S(1)}, u32[]{:S(2)}, u32[]{:S(2)}) collective-permute-start(bf16[528,128]{1,0:T(8,128)(2,1)} %get-tuple-element.22), channel_id=1, source_target_pairs={{0,64},{8,72},{16,80},{24,88},{32,96},{40,104},{48,112},{56,120},{... | collective-permute-start | bytes 405512 | tf_op jit(solution)/shard_map/ppermute | solution.py:521
  71.9 8.4 %collective-permute-start.5 = (bf16[528,128]{1,0:T(8,128)(2,1)}, bf16[528,128]{1,0:T(8,128)(2,1)S(1)}, u32[]{:S(2)}, u32[]{:S(2)}) collective-permute-start(bf16[528,128]{1,0:T(8,128)(2,1)} %get-tuple-element.22), channel_id=1, source_target_pairs={{0,96},{8,104},{16,112},{24,120},{1,97},{9,105},{17,113},{25,121},... | collective-permute-start | bytes 405512 | tf_op jit(solution)/shard_map/ppermute | solution.py:521
  86.3 31.5 %collective-permute-start.7 = (bf16[1024,512]{1,0:T(8,128)(2,1)}, bf16[1024,512]{1,0:T(8,128)(2,1)}, u32[]{:S(2)}, u32[]{:S(2)}) collective-permute-start(bf16[1024,512]{1,0:T(8,128)(2,1)} %finish.1.refs_0_), channel_id=1, source_target_pairs={{0,2},{1,3},{2,4},{3,5},{4,6},{5,7},{6,0},{7,1},{8,10},{9,11},{10,... | collective-permute-start | bytes 3145736 | tf_op jit(solution)/shard_map/ppermute | solution.py:430
  86.3 34.0 %collective-permute-start.8 = (bf16[1024,512]{1,0:T(8,128)(2,1)}, bf16[1024,512]{1,0:T(8,128)(2,1)}, u32[]{:S(2)}, u32[]{:S(2)}) collective-permute-start(bf16[1024,512]{1,0:T(8,128)(2,1)} %finish.1.refs_0_), channel_id=1, source_target_pairs={{0,6},{1,7},{2,0},{3,1},{4,2},{5,3},{6,4},{7,5},{8,14},{9,15},{10,... | collective-permute-start | bytes 3145736 | tf_op jit(solution)/shard_map/ppermute | solution.py:430
  89.6 23.4 %all-to-all-start.2 = ((s32[8,1,128]{2,1,0:T(1,128)}), s32[8,1,128]{2,1,0:T(1,128)S(1)}, u32[]{:S(2)}, u32[]{:S(2)}) async-start(s32[8,1,128]{2,1,0:T(1,128)} %broadcast_in_dim.35), calls=%async_computation.2 | async-start | bytes 8192 | tf_op jit(solution)/shard_map/all_to_all | solution.py:532
  113.1 37.7 %all-to-all-start = ((bf16[128,8,768]{2,0,1:T(8,128)(2,1)}), bf16[128,8,768]{2,0,1:T(8,128)(2,1)S(1)}, u32[]{:S(2)}, u32[]{:S(2)}) async-start(bf16[128,8,768]{2,0,1:T(8,128)(2,1)} %bitcast.51), calls=%async_computation | async-start | bytes 3145728 | tf_op jit(solution)/shard_map/all_to_all | solution.py:530
  118.9 30.8 %collective-permute-start.11 = (bf16[1024,256]{1,0:T(8,128)(2,1)S(1)}, bf16[1024,256]{1,0:T(8,128)(2,1)}, u32[]{:S(2)}, u32[]{:S(2)}) collective-permute-start(bf16[1024,256]{1,0:T(8,128)(2,1)S(1)} %slice.16), channel_id=1, source_target_pairs={{0,2},{1,3},{2,4},{3,5},{4,6},{5,7},{6,0},{7,1},{8,10},{9,11},{10,... | collective-permute-start | bytes 1572872 | tf_op jit(solution)/shard_map/ppermute | solution.py:430
  122.2 28.2 %collective-permute-start.12 = (bf16[1024,256]{1,0:T(8,128)(2,1)}, bf16[1024,256]{1,0:T(8,128)(2,1)}, u32[]{:S(2)}, u32[]{:S(2)}) collective-permute-start(bf16[1024,256]{1,0:T(8,128)(2,1)} %slice.17), channel_id=1, source_target_pairs={{0,6},{1,7},{2,0},{3,1},{4,2},{5,3},{6,4},{7,5},{8,14},{9,15},{10,... | collective-permute-start | bytes 1572872 | tf_op jit(solution)/shard_map/ppermute | solution.py:430
  123.5 27.2 %collective-permute-start.6 = (bf16[1024,512]{1,0:T(8,128)(2,1)S(1)}, bf16[1024,512]{1,0:T(8,128)(2,1)}, u32[]{:S(2)}, u32[]{:S(2)}) collective-permute-start(bf16[1024,512]{1,0:T(8,128)(2,1)S(1)} %copy-done.3), channel_id=1, source_target_pairs={{0,1},{1,0},{2,3},{3,2},{4,5},{5,4},{6,7},{7,6},{8,9},{9,8},{10,11... | collective-permute-start | bytes 3145736 | tf_op jit(solution)/shard_map/ppermute | solution.py:430
  124.1 29.0 %collective-permute-start.10 = (bf16[1024,512]{1,0:T(8,128)(2,1)}, bf16[1024,512]{1,0:T(8,128)(2,1)}, u32[]{:S(2)}, u32[]{:S(2)}) collective-permute-start(bf16[1024,512]{1,0:T(8,128)(2,1)} %collective-permute-done.8.refs_3_), channel_id=1, source_target_pairs={{0,1},{1,0},{2,3},{3,2},{4,5},{5,4},{6,7},{7,6},{8,9},{9,8},{10,11... | collective-permute-start | bytes 3145736 | tf_op jit(solution)/shard_map/ppermute | solution.py:430
  124.1 29.0 %collective-permute-start.9 = (bf16[1024,512]{1,0:T(8,128)(2,1)}, bf16[1024,512]{1,0:T(8,128)(2,1)}, u32[]{:S(2)}, u32[]{:S(2)}) collective-permute-start(bf16[1024,512]{1,0:T(8,128)(2,1)} %collective-permute-done.7.refs_2_), channel_id=1, source_target_pairs={{0,1},{1,0},{2,3},{3,2},{4,5},{5,4},{6,7},{7,6},{8,9},{9,8},{10,11... | collective-permute-start | bytes 3145736 | tf_op jit(solution)/shard_map/ppermute | solution.py:430
  149.7 2.6 collective-permute-start.13
  150.5 2.6 collective-permute-start.14
  202.2 53.8 %copy-start = (bf16[16,80,768]{2,1,0:T(8,128)(2,1)}, bf16[16,80,768]{2,1,0:T(8,128)(2,1)S(1)}, u32[]{:S(2)}) copy-start(bf16[16,80,768]{2,1,0:T(8,128)(2,1)S(1)} %all_to_all.49) | copy-start | bytes 5898244
  202.2 44.1 %collective-permute-start.17 = (bf16[1280,768]{1,0:T(8,128)(2,1)S(1)}, bf16[1280,768]{1,0:T(8,128)(2,1)}, u32[]{:S(2)}, u32[]{:S(2)}) collective-permute-start(bf16[1280,768]{1,0:T(8,128)(2,1)S(1)} %bitcast.72), channel_id=1, source_target_pairs={{0,2},{1,3},{2,4},{3,5},{4,6},{5,7},{6,0},{7,1},{8,10},{9,11},{10,... | collective-permute-start | bytes 5898248 | tf_op jit(solution)/shard_map/ppermute | solution.py:430
  202.2 51.5 %collective-permute-start.19 = (bf16[1280,768]{1,0:T(8,128)(2,1)S(1)}, bf16[1280,768]{1,0:T(8,128)(2,1)}, u32[]{:S(2)}, u32[]{:S(2)}) collective-permute-start(bf16[1280,768]{1,0:T(8,128)(2,1)S(1)} %bitcast.73), channel_id=1, source_target_pairs={{0,6},{1,7},{2,0},{3,1},{4,2},{5,3},{6,4},{7,5},{8,14},{9,15},{10,... | collective-permute-start | bytes 5898248 | tf_op jit(solution)/shard_map/ppermute | solution.py:430
  204.9 81.8 %collective-permute-start.25 = (bf16[1280,768]{1,0:T(8,128)(2,1)S(1)}, bf16[1280,768]{1,0:T(8,128)(2,1)}, u32[]{:S(2)}, u32[]{:S(2)}) collective-permute-start(bf16[1280,768]{1,0:T(8,128)(2,1)S(1)} %bitcast.74), channel_id=1, source_target_pairs={{0,1},{1,0},{2,3},{3,2},{4,5},{5,4},{6,7},{7,6},{8,9},{9,8},{10,11... | collective-permute-start | bytes 5898248 | tf_op jit(solution)/shard_map/ppermute | solution.py:430
  207.8 56.6 %all-to-all-start.1 = ((bf16[8,128,768]{2,1,0:T(8,128)(2,1)}), bf16[8,128,768]{2,1,0:T(8,128)(2,1)S(1)}, u32[]{:S(2)}, u32[]{:S(2)}) async-start(bf16[8,128,768]{2,1,0:T(8,128)(2,1)} %bitcast.91), calls=%async_computation.1 | async-start | bytes 3145728 | tf_op jit(solution)/shard_map/all_to_all | solution.py:546
  211.4 52.4 %copy-start.13 = (f32[6144]{0:T(1024)S(1)}, f32[6144]{0:T(1024)}, u32[]{:S(2)}) copy-start(f32[6144]{0:T(1024)} %param.18) | copy-start | bytes 73732
  246.4 63.8 %collective-permute-start.23 = (bf16[1280,768]{1,0:T(8,128)(2,1)}, bf16[1280,768]{1,0:T(8,128)(2,1)}, u32[]{:S(2)}, u32[]{:S(2)}) collective-permute-start(bf16[1280,768]{1,0:T(8,128)(2,1)} %collective-permute-done.17.refs_0_), channel_id=1, source_target_pairs={{0,1},{1,0},{2,3},{3,2},{4,5},{5,4},{6,7},{7,6},{8,9},{9,8},{10,11... | collective-permute-start | bytes 5898248 | tf_op jit(solution)/shard_map/ppermute | solution.py:430
  253.8 56.4 %collective-permute-start.24 = (bf16[1280,768]{1,0:T(8,128)(2,1)}, bf16[1280,768]{1,0:T(8,128)(2,1)}, u32[]{:S(2)}, u32[]{:S(2)}) collective-permute-start(bf16[1280,768]{1,0:T(8,128)(2,1)} %collective-permute-done.19.refs_1_), channel_id=1, source_target_pairs={{0,1},{1,0},{2,3},{3,2},{4,5},{5,4},{6,7},{7,6},{8,9},{9,8},{10,11... | collective-permute-start | bytes 5898248 | tf_op jit(solution)/shard_map/ppermute | solution.py:430
  256.0 29.6 %collective-permute-start.18 = (bf16[1280,384]{1,0:T(8,128)(2,1)}, bf16[1280,384]{1,0:T(8,128)(2,1)}, u32[]{:S(2)}, u32[]{:S(2)}) collective-permute-start(bf16[1280,384]{1,0:T(8,128)(2,1)} %slice.18), channel_id=1, source_target_pairs={{0,2},{1,3},{2,4},{3,5},{4,6},{5,7},{6,0},{7,1},{8,10},{9,11},{10,... | collective-permute-start | bytes 2949128 | tf_op jit(solution)/shard_map/ppermute | solution.py:430
  258.3 28.4 %collective-permute-start.20 = (bf16[1280,384]{1,0:T(8,128)(2,1)}, bf16[1280,384]{1,0:T(8,128)(2,1)}, u32[]{:S(2)}, u32[]{:S(2)}) collective-permute-start(bf16[1280,384]{1,0:T(8,128)(2,1)} %slice.19), channel_id=1, source_target_pairs={{0,6},{1,7},{2,0},{3,1},{4,2},{5,3},{6,4},{7,5},{8,14},{9,15},{10,... | collective-permute-start | bytes 2949128 | tf_op jit(solution)/shard_map/ppermute | solution.py:430
  285.6 37.0 %collective-permute-start.21 = (bf16[1280,384]{1,0:T(8,128)(2,1)}, bf16[1280,384]{1,0:T(8,128)(2,1)S(1)}, u32[]{:S(2)}, u32[]{:S(2)}) collective-permute-start(bf16[1280,384]{1,0:T(8,128)(2,1)} %collective-permute-done.18.refs_0_), channel_id=1, source_target_pairs={{0,1},{1,0},{2,3},{3,2},{4,5},{5,4},{6,7},{7,6},{8,9},{9,8},{10,11... | collective-permute-start | bytes 2949128 | tf_op jit(solution)/shard_map/ppermute | solution.py:430
  286.7 35.9 %collective-permute-start.22 = (bf16[1280,384]{1,0:T(8,128)(2,1)}, bf16[1280,384]{1,0:T(8,128)(2,1)S(1)}, u32[]{:S(2)}, u32[]{:S(2)}) collective-permute-start(bf16[1280,384]{1,0:T(8,128)(2,1)} %collective-permute-done.20.refs_1_), channel_id=1, source_target_pairs={{0,1},{1,0},{2,3},{3,2},{4,5},{5,4},{6,7},{7,6},{8,9},{9,8},{10,11... | collective-permute-start | bytes 2949128 | tf_op jit(solution)/shard_map/ppermute | solution.py:430
  (13 other events, 60.4 us)
Sparse Core Ops, SparseCore 0:
  26.0 77.2 all-gather.1
